TPU v7x, 32 devices: a whole 2x2x4 slice. The times are simulated.
32 devices in a mesh: groups: 2 (over y), mesh: 8 (over z, x), noise: 2 (over core).
Axes of the slice: x: 2, y: 2, z: 4, core: 2. Of those that a mesh axis runs over, the one named last changes fastest.
Arguments:
- inputs: bfloat16 [4, 4096, 512], P(('groups', 'noise'), 'mesh'), parts along dimension 0, may hold values from -6 to 6
- norm_gain: float32 [512], replicated, may hold values from 0.1 to 1.9
- qkv_weight: bfloat16 [512, 1536], replicated, may hold values from -3 to 3
- neighbours: int32 [32, 6], replicated, may hold values from 0 to 31, as said below
- out_grad: bfloat16 [4, 4096, 512], P(('groups', 'noise'), 'mesh'), parts along dimension 0, may hold values from -6 to 6
Outputs:
- input_grad: bfloat16 [4, 4096, 512], P(('groups', 'noise'), 'mesh'), parts along dimension 0
- weight_grad: float32 [1024, 1536], P(('groups', 'mesh')), parts along dimension 0
- gain_grad: float32 [1024], P(('groups', 'mesh')), parts along dimension 0
There are 2 independent parts, one for each index of `groups`. A program takes and returns all parts, laid end to end along the dimension named above; an argument that names none is the same for every part. Nothing has to cross between parts.
Inputs may be any that keep to these rules, and one draw needn't show every extreme that they name: `neighbours`: row b lists block b first, then 6 - 1 other distinct blocks. Block c belongs to device c // 4 of mesh; every listed block belongs to a device at most 2 places away from the device of b. The blocks of one device list at most 2 distinct blocks of any one other device, and exactly 2 for some pair of devices.
All inputs are finite; a program needn't handle non-finite values.
Results may differ from a plain program's by a relative error of at most 0.0091.
Values may be sent and summed in bfloat16 or wider, within the bound.
A program may use at most 64 MiB of HBM per device.

v0:
```python
import math

import jax
import jax.numpy as jnp
from jax import lax
from jax.sharding import PartitionSpec as P

HEADS = 4
BS = 128
KHOP = 6
REACH = 2


EPSILON = 1e-05


def shifted(block, axis, distance):
    devices = range(lax.axis_size(axis))
    route = [(i - distance, i) for i in devices if i - distance in devices]
    return lax.ppermute(block, axis, route)


def per_device(inputs, norm_gain, qkv_weight, neighbours, out_grad):
    samples, row_count, features = inputs.shape
    blocks = row_count // BS
    head_dim = features // HEADS
    own_index = lax.axis_index("mesh")
    as_float = inputs.astype(jnp.float32)
    centred = as_float - jnp.mean(as_float, axis=-1, keepdims=True)
    inv_std = lax.rsqrt(jnp.mean(centred * centred, axis=-1, keepdims=True) + EPSILON)
    unit_rows = centred * inv_std
    normed = (unit_rows * norm_gain).astype(jnp.bfloat16)
    normed_rows = normed.reshape(samples * row_count, features)
    projected = jnp.dot(normed_rows, qkv_weight, preferred_element_type=jnp.float32).astype(
        jnp.bfloat16
    )
    projected = projected.reshape(samples, blocks, BS, 3, HEADS, head_dim)
    queries = projected[:, :, :, 0]
    own_pairs = projected[:, :, :, 1:]
    block_range = jnp.arange(blocks, dtype=jnp.int32)
    offsets = [shift_by for shift_by in range(-REACH, REACH + 1) if shift_by != 0]
    table_parts = [own_pairs]
    table_ids = [own_index * blocks + block_range]
    for offset in offsets:
        arrived = shifted(own_pairs, "mesh", -offset)
        table_parts.append(arrived)
        table_ids.append((own_index + offset) * blocks + block_range)
    table = jnp.concatenate(table_parts, axis=1)
    all_ids = jnp.concatenate(table_ids, axis=0)
    my_rows = lax.dynamic_slice_in_dim(neighbours, own_index * blocks, blocks, 0)
    matches = my_rows[:, :, None] == all_ids[None, None, :]
    where_from = jnp.sum(matches * jnp.arange(all_ids.shape[0], dtype=jnp.int32), axis=2)
    table_hits = matches.astype(jnp.float32)
    score_scale = 1.0 / math.sqrt(head_dim)

    def per_head(members):
        query_head, pair_head, grad_head = members
        gathered = pair_head[:, where_from]
        key_part = gathered[:, :, :, :, 0]
        value_part = gathered[:, :, :, :, 1]
        scores = (
            jnp.einsum(
                "sbqd,sbjkd->sbqjk", query_head, key_part, preferred_element_type=jnp.float32
            )
            * score_scale
        )
        flat_scores = scores.reshape(samples, blocks, BS, KHOP * BS)
        row_max = jnp.max(flat_scores, axis=-1, keepdims=True)
        powers = jnp.exp(flat_scores - row_max)
        attend = (powers / jnp.sum(powers, axis=-1, keepdims=True)).reshape(scores.shape)
        attend_low = attend.astype(jnp.bfloat16)
        attended = jnp.einsum(
            "sbqjk,sbjkd->sbqd", attend_low, value_part, preferred_element_type=jnp.float32
        )
        row_dot = jnp.sum(grad_head.astype(jnp.float32) * attended, axis=-1)
        grad_attend = jnp.einsum(
            "sbqd,sbjkd->sbqjk", grad_head, value_part, preferred_element_type=jnp.float32
        )
        grad_scores = attend * (grad_attend - row_dot[..., None, None])
        grad_low = grad_scores.astype(jnp.bfloat16)
        query_grad = (
            jnp.einsum("sbqjk,sbjkd->sbqd", grad_low, key_part, preferred_element_type=jnp.float32)
            * score_scale
        )
        key_grad = (
            jnp.einsum(
                "sbqjk,sbqd->sbjkd", grad_low, query_head, preferred_element_type=jnp.float32
            )
            * score_scale
        )
        value_grad = jnp.einsum(
            "sbqjk,sbqd->sbjkd", attend_low, grad_head, preferred_element_type=jnp.float32
        )
        pair_grad = jnp.stack([key_grad, value_grad], axis=4)
        partials = jnp.einsum(
            "bjt,sbjkcd->stkcd", table_hits, pair_grad, precision=lax.Precision.HIGHEST
        )
        return (query_grad, partials.astype(jnp.bfloat16))

    query_heads = queries.transpose(3, 0, 1, 2, 4)
    pair_heads = table.transpose(4, 0, 1, 2, 3, 5)
    grad_heads = out_grad.reshape(samples, blocks, BS, HEADS, head_dim).transpose(3, 0, 1, 2, 4)
    query_grads, partials = lax.map(per_head, (query_heads, pair_heads, grad_heads))
    query_grads = query_grads.transpose(1, 2, 3, 0, 4)
    partials = partials.transpose(1, 2, 3, 4, 0, 5)
    pair_total = partials[:, :blocks].astype(jnp.float32)
    for number, offset in enumerate(offsets):
        start = blocks * (number + 1)
        returned = shifted(partials[:, start : start + blocks], "mesh", offset)
        pair_total = pair_total + returned.astype(jnp.float32)
    grad_rows = jnp.concatenate([query_grads[:, :, :, None], pair_total], axis=3)
    grad_rows = grad_rows.astype(jnp.bfloat16).reshape(samples * row_count, 3 * features)
    grad_scale = 1.0 / math.sqrt(
        samples * row_count * lax.axis_size("mesh") * lax.axis_size("noise")
    )
    weight_term = (
        lax.dot_general(
            normed_rows, grad_rows, (((0,), (0,)), ((), ())), preferred_element_type=jnp.float32
        )
        * grad_scale
    )
    normed_grad = lax.dot_general(
        grad_rows, qkv_weight, (((1,), (1,)), ((), ())), preferred_element_type=jnp.float32
    ).reshape(samples, row_count, features)
    gain_term = jnp.sum(normed_grad * unit_rows, axis=(0, 1)) * grad_scale
    unit_grad = normed_grad * norm_gain
    input_grad = inv_std * (
        unit_grad
        - jnp.mean(unit_grad, axis=-1, keepdims=True)
        - unit_rows * jnp.mean(unit_grad * unit_rows, axis=-1, keepdims=True)
    )
    weight_all, gain_all = (
        lax.psum(weight_term.astype(jnp.bfloat16), "noise").astype(jnp.float32),
        lax.psum(gain_term.astype(jnp.bfloat16), "noise").astype(jnp.float32),
    )
    weight_grad, gain_grad = (
        lax.psum_scatter(weight_all, "mesh", scatter_dimension=0, tiled=True),
        lax.psum_scatter(gain_all, "mesh", scatter_dimension=0, tiled=True),
    )
    return (input_grad.astype(jnp.bfloat16), weight_grad, gain_grad)


def solution(mesh):
    return jax.shard_map(
        per_device,
        mesh=mesh,
        in_specs=(
            P(("groups", "noise"), "mesh", None),
            P(),
            P(),
            P(),
            P(("groups", "noise"), "mesh", None),
        ),
        out_specs=(
            P(("groups", "noise"), "mesh", None),
            P(("groups", "mesh"), None),
            P(("groups", "mesh")),
        ),
        check_vma=False,
    )
```

profile of v0, /device:TPU:0, one launch (start us, length us, event | category | flops | bytes accessed | tf_op | source)
XLA Modules:
  0.0 331.8 jit_solution(5239867428918473955)
XLA Ops:
  7.2 1.4 copy.57
  8.9 2.3 convolution_convert_fusion
  11.2 4.0 %reshape.208 = bf16[1,4,128,3,4,128]{5,4,3,2,1,0:T(4,128)(2,1)} reshape(bf16[512,1536]{1,0:T(8,128)(2,1)} %convolution_convert_fusion) | data formatting | bytes 3145728 | tf_op jit(solution)/shard_map/reshape | solution.py:37
  16.4 1.8 fusion.53
  18.2 6.0 %collective-permute-start = (bf16[1,4,128,2,4,128]{5,2,3,1,0,4:T(8,128)(2,1)}, bf16[1,4,128,2,4,128]{5,2,3,1,0,4:T(8,128)(2,1)}, u32[]{:S(2)}, u32[]{:S(2)}) collective-permute-start(bf16[1,4,128,2,4,128]{5,2,3,1,0,4:T(8,128)(2,1)} %get-tuple-element.135), channel_id=1, source_target_pairs={{0,4},{2,6},{4,8},{6,10},{8,12},{10,14},{1,5},{3,7},{5,9},{7,11},{... | collective-permute-start | bytes 3145736 | tf_op jit(solution)/shard_map/ppermute | solution.py:20
  24.2 4.4 %collective-permute-start.1 = (bf16[1,4,128,2,4,128]{5,2,3,1,0,4:T(8,128)(2,1)}, bf16[1,4,128,2,4,128]{5,2,3,1,0,4:T(8,128)(2,1)}, u32[]{:S(2)}, u32[]{:S(2)}) collective-permute-start(bf16[1,4,128,2,4,128]{5,2,3,1,0,4:T(8,128)(2,1)} %get-tuple-element.135), channel_id=1, source_target_pairs={{0,2},{2,4},{4,6},{6,8},{8,10},{10,12},{12,14},{1,3},{3,5},{5,7},{... | collective-permute-start | bytes 3145736 | tf_op jit(solution)/shard_map/ppermute | solution.py:20
  29.9 1.5 collective-permute-start.3
  35.2 10.8 %collective-permute-done = bf16[1,4,128,2,4,128]{5,2,3,1,0,4:T(8,128)(2,1)} collective-permute-done((bf16[1,4,128,2,4,128]{5,2,3,1,0,4:T(8,128)(2,1)}, bf16[1,4,128,2,4,128]{5,2,3,1,0,4:T(8,128)(2,1)}, u32[]{:S(2)}, u32[]{:S(2)}) %collective-permute-start) | collective-permute-done | bytes 1048608 | tf_op jit(solution)/shard_map/ppermute | solution.py:20
  46.0 2.5 constant_dynamic-update-slice_fusion.3
  48.5 24.1 %collective-permute-done.1 = bf16[1,4,128,2,4,128]{5,2,3,1,0,4:T(8,128)(2,1)} collective-permute-done((bf16[1,4,128,2,4,128]{5,2,3,1,0,4:T(8,128)(2,1)}, bf16[1,4,128,2,4,128]{5,2,3,1,0,4:T(8,128)(2,1)}, u32[]{:S(2)}, u32[]{:S(2)}) %collective-permute-start.1) | collective-permute-done | bytes 1048608 | tf_op jit(solution)/shard_map/ppermute | solution.py:20
  72.5 2.5 constant_dynamic-update-slice_fusion.2
  75.0 2.5 constant_dynamic-update-slice_fusion.1
  77.5 2.5 constant_dynamic-update-slice_fusion
  80.0 72.6 %while.13 = (s32[]{:T(128)}, bf16[4,1,4,128,128]{4,2,3,0,1:T(4,128)(2,1)}, bf16[4,1,20,128,2,128]{5,2,4,3,1,0:T(8,128)(2,1)}, bf16[4,1,4,128,128]{4,3,2,1,0:T(8,...) while((s32[]{:T(128)}, ...), condition=%wide.region_7.8_spmd.clone, body=%wide.region_3.7_spmd.clone.sunk | while | flops 800784896 | bytes 41708468 | solution.py:103
  80.0 1.4 dynamic-slice_bitcast_fusion.2
  81.6 2.0 gather_fusion
  83.5 1.6 copy.104
  89.5 8.7 %bitcast_dynamic-update-slice_fusion.2 = bf16[4,1,20,128,2,128]{5,2,4,3,1,0:T(8,128)(2,1)} fusion(bf16[4,1,20,128,2,128]{5,2,4,3,1,0:T(8,128)(2,1)} %get-tuple-element.213, s32[]{:T(128)S(6)} %copy.114, f32[4,6,128,2,128]{4,2,1,0,3:T(8,128)S(1)} %maximum_bitcast_fusion.2, s32[20]{0:T(128)S(1)} %get-tuple-element.228, s32[4,6]{1,0:T(4,128)S(1)} %get-tuple-element.229), kind=kOutput, calls=%fused_computation.6.clone.1 | convolution fusion | flops 189400000 | bytes 4718772 | tf_op jit(solution)/shard_map/while/body/eval_jaxpr/bjt,sbjkcd->stkcd/dot_general | solution.py:95
  98.2 1.4 dynamic-slice_bitcast_fusion.2
  99.7 2.0 gather_fusion
  101.7 1.6 copy.104
  107.7 8.7 %bitcast_dynamic-update-slice_fusion.2 = bf16[4,1,20,128,2,128]{5,2,4,3,1,0:T(8,128)(2,1)} fusion(bf16[4,1,20,128,2,128]{5,2,4,3,1,0:T(8,128)(2,1)} %get-tuple-element.213, s32[]{:T(128)S(6)} %copy.114, f32[4,6,128,2,128]{4,2,1,0,3:T(8,128)S(1)} %maximum_bitcast_fusion.2, s32[20]{0:T(128)S(1)} %get-tuple-element.228, s32[4,6]{1,0:T(4,128)S(1)} %get-tuple-element.229), kind=kOutput, calls=%fused_computation.6.clone.1 | convolution fusion | flops 189400000 | bytes 4718772 | tf_op jit(solution)/shard_map/while/body/eval_jaxpr/bjt,sbjkcd->stkcd/dot_general | solution.py:95
  116.4 1.4 dynamic-slice_bitcast_fusion.2
  117.9 2.0 gather_fusion
  119.9 1.6 copy.104
  125.8 8.7 %bitcast_dynamic-update-slice_fusion.2 = bf16[4,1,20,128,2,128]{5,2,4,3,1,0:T(8,128)(2,1)} fusion(bf16[4,1,20,128,2,128]{5,2,4,3,1,0:T(8,128)(2,1)} %get-tuple-element.213, s32[]{:T(128)S(6)} %copy.114, f32[4,6,128,2,128]{4,2,1,0,3:T(8,128)S(1)} %maximum_bitcast_fusion.2, s32[20]{0:T(128)S(1)} %get-tuple-element.228, s32[4,6]{1,0:T(4,128)S(1)} %get-tuple-element.229), kind=kOutput, calls=%fused_computation.6.clone.1 | convolution fusion | flops 189400000 | bytes 4718772 | tf_op jit(solution)/shard_map/while/body/eval_jaxpr/bjt,sbjkcd->stkcd/dot_general | solution.py:95
  134.5 1.4 dynamic-slice_bitcast_fusion.2
  136.0 2.0 gather_fusion
  138.0 1.6 copy.104
  144.0 8.7 %bitcast_dynamic-update-slice_fusion.2 = bf16[4,1,20,128,2,128]{5,2,4,3,1,0:T(8,128)(2,1)} fusion(bf16[4,1,20,128,2,128]{5,2,4,3,1,0:T(8,128)(2,1)} %get-tuple-element.213, s32[]{:T(128)S(6)} %copy.114, f32[4,6,128,2,128]{4,2,1,0,3:T(8,128)S(1)} %maximum_bitcast_fusion.2, s32[20]{0:T(128)S(1)} %get-tuple-element.228, s32[4,6]{1,0:T(4,128)S(1)} %get-tuple-element.229), kind=kOutput, calls=%fused_computation.6.clone.1 | convolution fusion | flops 189400000 | bytes 4718772 | tf_op jit(solution)/shard_map/while/body/eval_jaxpr/bjt,sbjkcd->stkcd/dot_general | solution.py:95
  152.7 4.2 %fusion.52 = (bf16[1,4,128,2,4,128]{5,1,3,2,0,4:T(4,128)(2,1)S(1)}, bf16[1,4,128,2,4,128]{5,1,3,2,0,4:T(4,128)(2,1)S(1)}, bf16[1,4,128,2,4,128]{5,1,3,2,0,4:T(4,128)(2,1)S(1)}, bf16[1,4,128,2,4,128]{5,1,3,2,0,4:T(4,128)(2,1)S(1)}) fusion(bf16[1,20,128,2,4,128]{5,1,3,2,0,4:T(8,128)(2,1)} %bitcast.155), kind=kLoop, calls=%fused_computation.85 | loop fusion | bytes 8388608 | tf_op jit(solution)/shard_map/slice | solution.py:109
  156.9 4.2 %collective-permute-start.7 = (bf16[1,4,128,2,4,128]{5,1,3,2,0,4:T(4,128)(2,1)S(1)}, bf16[1,4,128,2,4,128]{5,1,3,2,0,4:T(4,128)(2,1)S(1)}, u32[]{:S(2)}, u32[]{:S(2)}) collective-permute-start(bf16[1,4,128,2,4,128]{5,1,3,2,0,4:T(4,128)(2,1)S(1)} %get-tuple-element.132), channel_id=1, source_target_pairs={{0,4},{2,6},{4,8},{6,10},{8,12},{10,14},{1,5},{3,7},{5,9},{7,11},{... | collective-permute-start | bytes 3145736 | tf_op jit(solution)/shard_map/ppermute | solution.py:20
  161.1 2.9 collective-permute-start.6
  164.0 1.3 collective-permute-start.5
  165.3 1.6 collective-permute-start.4
  167.0 15.0 %collective-permute-done.7 = bf16[1,4,128,2,4,128]{5,1,3,2,0,4:T(4,128)(2,1)S(1)} collective-permute-done((bf16[1,4,128,2,4,128]{5,1,3,2,0,4:T(4,128)(2,1)S(1)}, bf16[1,4,128,2,4,128]{5,1,3,2,0,4:T(4,128)(2,1)S(1)}, u32[]{:S(2)}, u32[]{:S(2)}) %collective-permute-start.7) | collective-permute-done | bytes 1048608 | tf_op jit(solution)/shard_map/ppermute | solution.py:20
  182.0 25.3 %collective-permute-done.6 = bf16[1,4,128,2,4,128]{5,1,3,2,0,4:T(4,128)(2,1)S(1)} collective-permute-done((bf16[1,4,128,2,4,128]{5,1,3,2,0,4:T(4,128)(2,1)S(1)}, bf16[1,4,128,2,4,128]{5,1,3,2,0,4:T(4,128)(2,1)S(1)}, u32[]{:S(2)}, u32[]{:S(2)}) %collective-permute-start.6) | collective-permute-done | bytes 1048608 | tf_op jit(solution)/shard_map/ppermute | solution.py:20
  207.3 5.4 %collective-permute-done.4 = bf16[1,4,128,2,4,128]{5,1,3,2,0,4:T(4,128)(2,1)S(1)} collective-permute-done((bf16[1,4,128,2,4,128]{5,1,3,2,0,4:T(4,128)(2,1)S(1)}, bf16[1,4,128,2,4,128]{5,1,3,2,0,4:T(4,128)(2,1)S(1)}, u32[]{:S(2)}, u32[]{:S(2)}) %collective-permute-start.4) | collective-permute-done | bytes 1048608 | tf_op jit(solution)/shard_map/ppermute | solution.py:20
  212.7 2.9 convert_add_fusion
  216.8 2.4 copy.65
  219.1 3.8 %convert_element_type.99 = bf16[512,1536]{1,0:T(8,128)(2,1)} reshape(bf16[1,4,128,3,4,128]{5,4,3,2,1,0:T(4,128)(2,1)} %copy.65) | data formatting | bytes 3145728 | tf_op jit(solution)/shard_map/convert_element_type | solution.py:112
  223.0 3.6 %fusion.34 = bf16[512,1536]{1,0:T(8,128)(2,1)} fusion(bf16[512,1536]{1,0:T(8,128)(2,1)} %convert_element_type.99, bf16[1,512,512]{1,2,0:T(8,128)(2,1)S(1)} %copy.57, f32[512]{0:T(512)S(1)} %copy-done.5, f32[512]{0:T(512)S(1)} %add_rsqrt_fusion, f32[512]{0:T(512)S(1)} %broadcast_multiply_fusion.2), kind=kOutput, calls=%fused_computation.47 | convolution fusion | flops 808189952 | bytes 3676160 | tf_op jit(solution)/shard_map/dot_general | solution.py:117
  226.6 17.8 %all-reduce.3.cloned.1.call-done = bf16[512,1536]{1,0:T(8,128)(2,1)} async-done(((bf16[512,1536]{1,0:T(8,128)(2,1)}), bf16[512,1536]{1,0:T(8,128)(2,1)}) %all-reduce.3.cloned.1.call-update) | async-done | bytes 1572880 | tf_op jit(solution)/shard_map/psum | solution.py:133
  244.4 3.5 %convert_element_type.102 = f32[512,1536]{1,0:T(8,128)} convert(bf16[512,1536]{1,0:T(8,128)(2,1)} %all-reduce.3.cloned.1.call-done) | non-fusion elementwise | flops 786432 | bytes 4718592 | tf_op jit(solution)/shard_map/convert_element_type | solution.py:133
  249.8 2.6 fusion.46
  253.9 2.4 psum.15
  256.3 21.9 %all-reduce = f32[512]{0:T(512)S(1)} all-reduce(bf16[512]{0:T(512)(128)(2,1)S(1)} %psum.15), channel_id=3, replica_groups=mesh['groups'=2,'mesh'=8,'noise'=2] {'mesh'}, use_global_device_ids=true, to_apply=%region_14.15.clone | all-reduce | flops 512 | bytes 3072
  278.8 46.1 %reduce-scatter.2.cloned.1.call-done = f32[64,1536]{1,0:T(8,128)} async-done(((f32[512,1536]{1,0:T(8,128)}), f32[64,1536]{1,0:T(8,128)}) %reduce-scatter.2.cloned.1.call-update) | async-done | bytes 393232 | tf_op jit(solution)/shard_map/reduce_scatter | solution.py:137
  (113 shorter events, 28.9 us)
Async XLA Ops:
  7.2 1.7 copy-start
  7.2 1.7 copy-start.5
  7.2 237.2 %all-reduce.3.cloned.1.call-start = ((), (), s32[]{:S(2)}) async-start(), calls=%async_computation.1 | async-start | bytes 3145728 | tf_op jit(solution)/shard_map/psum | solution.py:133
  15.1 1.2 slice-start
  18.2 15.4 %copy-start.6 = (s32[32,6]{0,1:T(8,128)S(1)}, s32[32,6]{0,1:T(8,128)}, u32[]{:S(2)}) copy-start(s32[32,6]{0,1:T(8,128)} %param.10) | copy-start | bytes 2308
  18.2 16.0 %copy-start.2 = (bf16[1,512,512]{2,1,0:T(8,128)(2,1)S(1)}, bf16[1,512,512]{2,1,0:T(8,128)(2,1)}, u32[]{:S(2)}) copy-start(bf16[1,512,512]{2,1,0:T(8,128)(2,1)} %param.11) | copy-start | bytes 1572868
  18.2 27.8 %collective-permute-start = (bf16[1,4,128,2,4,128]{5,2,3,1,0,4:T(8,128)(2,1)}, bf16[1,4,128,2,4,128]{5,2,3,1,0,4:T(8,128)(2,1)}, u32[]{:S(2)}, u32[]{:S(2)}) collective-permute-start(bf16[1,4,128,2,4,128]{5,2,3,1,0,4:T(8,128)(2,1)} %get-tuple-element.135), channel_id=1, source_target_pairs={{0,4},{2,6},{4,8},{6,10},{8,12},{10,14},{1,5},{3,7},{5,9},{7,11},{... | collective-permute-start | bytes 3145736 | tf_op jit(solution)/shard_map/ppermute | solution.py:20
  24.2 48.3 %collective-permute-start.1 = (bf16[1,4,128,2,4,128]{5,2,3,1,0,4:T(8,128)(2,1)}, bf16[1,4,128,2,4,128]{5,2,3,1,0,4:T(8,128)(2,1)}, u32[]{:S(2)}, u32[]{:S(2)}) collective-permute-start(bf16[1,4,128,2,4,128]{5,2,3,1,0,4:T(8,128)(2,1)} %get-tuple-element.135), channel_id=1, source_target_pairs={{0,2},{2,4},{4,6},{6,8},{8,10},{10,12},{12,14},{1,3},{3,5},{5,7},{... | collective-permute-start | bytes 3145736 | tf_op jit(solution)/shard_map/ppermute | solution.py:20
  28.6 46.4 %collective-permute-start.2 = (bf16[1,4,128,2,4,128]{5,2,3,1,0,4:T(8,128)(2,1)}, bf16[1,4,128,2,4,128]{5,2,3,1,0,4:T(8,128)(2,1)}, u32[]{:S(2)}, u32[]{:S(2)}) collective-permute-start(bf16[1,4,128,2,4,128]{5,2,3,1,0,4:T(8,128)(2,1)} %get-tuple-element.135), channel_id=1, source_target_pairs={{2,0},{4,2},{6,4},{8,6},{10,8},{12,10},{14,12},{3,1},{5,3},{7,5},{... | collective-permute-start | bytes 3145736 | tf_op jit(solution)/shard_map/ppermute | solution.py:20
  29.9 47.6 %collective-permute-start.3 = (bf16[1,4,128,2,4,128]{5,2,3,1,0,4:T(8,128)(2,1)}, bf16[1,4,128,2,4,128]{5,2,3,1,0,4:T(8,128)(2,1)}, u32[]{:S(2)}, u32[]{:S(2)}) collective-permute-start(bf16[1,4,128,2,4,128]{5,2,3,1,0,4:T(8,128)(2,1)} %get-tuple-element.135), channel_id=1, source_target_pairs={{4,0},{6,2},{8,4},{10,6},{12,8},{14,10},{5,1},{7,3},{9,5},{11,7},{... | collective-permute-start | bytes 3145736 | tf_op jit(solution)/shard_map/ppermute | solution.py:20
  83.5 1.6 copy-start.1
  85.1 1.0 copy-start.3
  101.7 1.6 copy-start.1
  103.3 1.0 copy-start.3
  119.9 1.6 copy-start.1
  121.4 1.0 copy-start.3
  138.0 1.6 copy-start.1
  139.6 1.0 copy-start.3
  156.9 25.0 %collective-permute-start.7 = (bf16[1,4,128,2,4,128]{5,1,3,2,0,4:T(4,128)(2,1)S(1)}, bf16[1,4,128,2,4,128]{5,1,3,2,0,4:T(4,128)(2,1)S(1)}, u32[]{:S(2)}, u32[]{:S(2)}) collective-permute-start(bf16[1,4,128,2,4,128]{5,1,3,2,0,4:T(4,128)(2,1)S(1)} %get-tuple-element.132), channel_id=1, source_target_pairs={{0,4},{2,6},{4,8},{6,10},{8,12},{10,14},{1,5},{3,7},{5,9},{7,11},{... | collective-permute-start | bytes 3145736 | tf_op jit(solution)/shard_map/ppermute | solution.py:20
  161.1 46.2 %collective-permute-start.6 = (bf16[1,4,128,2,4,128]{5,1,3,2,0,4:T(4,128)(2,1)S(1)}, bf16[1,4,128,2,4,128]{5,1,3,2,0,4:T(4,128)(2,1)S(1)}, u32[]{:S(2)}, u32[]{:S(2)}) collective-permute-start(bf16[1,4,128,2,4,128]{5,1,3,2,0,4:T(4,128)(2,1)S(1)} %get-tuple-element.133), channel_id=1, source_target_pairs={{0,2},{2,4},{4,6},{6,8},{8,10},{10,12},{12,14},{1,3},{3,5},{5,7},{... | collective-permute-start | bytes 3145736 | tf_op jit(solution)/shard_map/ppermute | solution.py:20
  164.0 43.3 %collective-permute-start.5 = (bf16[1,4,128,2,4,128]{5,1,3,2,0,4:T(4,128)(2,1)S(1)}, bf16[1,4,128,2,4,128]{5,1,3,2,0,4:T(4,128)(2,1)S(1)}, u32[]{:S(2)}, u32[]{:S(2)}) collective-permute-start(bf16[1,4,128,2,4,128]{5,1,3,2,0,4:T(4,128)(2,1)S(1)} %get-tuple-element.134), channel_id=1, source_target_pairs={{2,0},{4,2},{6,4},{8,6},{10,8},{12,10},{14,12},{3,1},{5,3},{7,5},{... | collective-permute-start | bytes 3145736 | tf_op jit(solution)/shard_map/ppermute | solution.py:20
  165.3 50.4 %copy-start.4 = (bf16[4,1,4,128,128]{4,2,3,0,1:T(4,128)(2,1)S(1)}, bf16[4,1,4,128,128]{4,2,3,0,1:T(4,128)(2,1)}, u32[]{:S(2)}) copy-start(bf16[4,1,4,128,128]{4,2,3,0,1:T(4,128)(2,1)} %get-tuple-element.46) | copy-start | bytes 1572868
  165.3 47.4 %collective-permute-start.4 = (bf16[1,4,128,2,4,128]{5,1,3,2,0,4:T(4,128)(2,1)S(1)}, bf16[1,4,128,2,4,128]{5,1,3,2,0,4:T(4,128)(2,1)S(1)}, u32[]{:S(2)}, u32[]{:S(2)}) collective-permute-start(bf16[1,4,128,2,4,128]{5,1,3,2,0,4:T(4,128)(2,1)S(1)} %get-tuple-element.131), channel_id=1, source_target_pairs={{4,0},{6,2},{8,4},{10,6},{12,8},{14,10},{5,1},{7,3},{9,5},{11,7},{... | collective-permute-start | bytes 3145736 | tf_op jit(solution)/shard_map/ppermute | solution.py:20
  226.6 98.3 %reduce-scatter.2.cloned.1.call-start = ((), (), s32[]{:S(2)}) async-start(), calls=%async_computation.2 | async-start | bytes 3538944 | tf_op jit(solution)/shard_map/reduce_scatter | solution.py:137
  247.9 0.7 copy-start.7
Sparse Core Ops, SparseCore 0:
  226.7 17.6 all-reduce.2
  249.0 75.8 reduce-scatter.1
where the time goes:
time: 333 us; the launch traced here: 332 us
  waiting for transfers between devices  144 us (43%)
  local copies, waits for them, and re-layouts  60 us (18%)
  matrix products  53.6 us (16%)
  blocking collectives  24.4 us (7%)
  starting transfers between devices  23.2 us (7%)
  between operations  14.9 us (4%)
  other arithmetic  10.9 us (3%)
    ppermute x8, waiting for transfers between devices, shifted(): return lax.ppermute(block, axis, route)  80.6 us
    reduce_scatter x1, waiting for transfers between devices, per_device(): lax.psum_scatter(weight_all, 'mesh', scatter_dimension=0, tiled=True)  46.1 us
    dot_general x4, matrix products, per_head(): jnp.einsum('bjt,sbjkcd->stkcd', table_hits, pair_grad, precision=lax.Prec...  34.8 us
    ppermute x8, starting transfers between devices, shifted(): return lax.ppermute(block, axis, route)  23.2 us
    unnamed x1, blocking collectives  21.9 us
    psum x1, waiting for transfers between devices, per_device(): lax.psum(weight_term.astype(jnp.bfloat16), 'noise').astype(jnp.float32)  17.8 us
    unnamed x24, local copies, waits for them, and re-layouts  15.5 us
    gather x8, local copies, waits for them, and re-layouts, per_head(): gathered = pair_head[:, where_from]  14.2 us
  transfers between devices with their start and end apart: 10, of which 7 were waited for; matrix products, arithmetic and copies ran while one was open for 5% of the time, Pallas kernels for 0%

commit v1 on v0

v1 whole, which is shorter than its diff:
```python
import functools
import math

import jax
import jax.numpy as jnp
from jax import lax
from jax.experimental import pallas as pl
from jax.experimental.pallas import tpu as pltpu
from jax.sharding import PartitionSpec as P

HEADS = 4
BS = 128
KHOP = 6
BLK = 4
CAP = 2
EPSILON = 1e-05
OFFSETS = (-2, -1, 1, 2)
TABLE = BLK + CAP * len(OFFSETS)
MESH = pl.DeviceIdType.MESH
F32 = jnp.float32
BF16 = jnp.bfloat16


def dot(a, b, dims):
    return lax.dot_general(a, b, (dims, ((), ())), preferred_element_type=F32)


def layer_norm(rows):
    as_float = rows.astype(F32)
    centred = as_float - jnp.mean(as_float, axis=-1, keepdims=True)
    inv_std = lax.rsqrt(jnp.mean(centred * centred, axis=-1, keepdims=True) + EPSILON)
    return centred * inv_std, inv_std


def pick_two(hits):
    first = jnp.int32(BLK - 1)
    for c in reversed(range(BLK - 1)):
        first = jnp.where(hits[c], c, first)
    second = jnp.int32(0)
    for c in reversed(range(1, BLK)):
        second = jnp.where(jnp.logical_and(hits[c], first < c), c, second)
    return first, second


def listed_flags(rows, device):
    flags = []
    for c in range(BLK):
        flag = rows[0] == device * BLK + c
        for entry in rows[1:]:
            flag = jnp.logical_or(flag, entry == device * BLK + c)
        flags.append(flag)
    return flags


def kernel(
    n, grad_scale, fused_sum,
    neigh, x, gain, w, og,
    *refs,
):
    outs, scratch = refs[:3], refs[3:]
    dx, w_out, gain_out = outs
    (send, halo, unit, inv, normed_t, q, kv, dq, dkv, terms, own_ng, ret_send, ret,
     halo_ss, halo_rs, ret_ss, ret_rs) = scratch[:17]
    me = lax.axis_index("mesh")
    core = lax.axis_index("noise")
    d = x.shape[-1]
    hd = d // HEADS
    rows_dev = BLK * BS
    scale = 1.0 / math.sqrt(hd)
    rows_out = d // n

    def exists(oi):
        other = me + OFFSETS[oi]
        return jnp.logical_and(other >= 0, other < n)

    barrier = pltpu.get_barrier_semaphore()
    if fused_sum:
        for k in range(1, n):
            pl.semaphore_signal(barrier, inc=1, device_id={"mesh": lax.rem(me + k, n)}, device_id_type=MESH)
        pl.semaphore_signal(barrier, inc=1, device_id={"noise": 1 - core}, device_id_type=MESH)
    else:
        for oi in range(len(OFFSETS)):
            @pl.when(exists(oi))
            def _():
                pl.semaphore_signal(barrier, inc=1, device_id={"mesh": me + OFFSETS[oi]}, device_id_type=MESH)

    wanted = []
    for oi, off in enumerate(OFFSETS):
        other = jnp.clip(me + off, 0, n - 1)
        entries = [neigh[other * BLK + b, j] for b in range(BLK) for j in range(KHOP)]
        flags = listed_flags(entries, me)
        first, second = pick_two(flags)
        wanted.append((flags, first, second))
        send[oi, 0] = x[first]
        send[oi, 1] = x[second]

    if fused_sum:
        pl.semaphore_wait(barrier, n)
    else:
        for oi in range(len(OFFSETS)):
            @pl.when(exists(oi))
            def _():
                pl.semaphore_wait(barrier, 1)

    def halo_copy(oi):
        return pltpu.make_async_remote_copy(
            src_ref=send.at[oi], dst_ref=halo.at[3 - oi],
            send_sem=halo_ss.at[oi], recv_sem=halo_rs.at[3 - oi],
            device_id={"mesh": me + OFFSETS[oi]}, device_id_type=MESH)

    def halo_arrival(oi):
        return pltpu.make_async_remote_copy(
            src_ref=send.at[oi], dst_ref=halo.at[oi],
            send_sem=halo_ss.at[oi], recv_sem=halo_rs.at[oi],
            device_id={"mesh": me + OFFSETS[oi]}, device_id_type=MESH)

    for oi in (0, 3, 1, 2):
        @pl.when(exists(oi))
        def _():
            halo_copy(oi).start()

        @pl.when(jnp.logical_not(exists(oi)))
        def _():
            halo[oi] = jnp.zeros(halo.shape[1:], BF16)

    mine = [[neigh[me * BLK + b, j] for j in range(KHOP)] for b in range(BLK)]
    flat = [entry for row in mine for entry in row]
    table_id = [me * BLK + c for c in range(BLK)]
    for oi, off in enumerate(OFFSETS):
        flags = listed_flags(flat, me + off)
        first, second = pick_two(flags)
        base = (me + off) * BLK
        table_id.append(jnp.where(functools.reduce(jnp.logical_or, flags), base + first, -1))
        table_id.append(jnp.where(second > 0, base + second, -1))
    where_from = [[None] * KHOP for _ in range(BLK)]
    back = [[None] * BLK for _ in range(TABLE)]
    none = BLK * KHOP
    for b in range(BLK):
        spots = [jnp.int32(0)] * KHOP
        for t in range(TABLE):
            found = jnp.int32(none)
            for j in range(KHOP):
                same = mine[b][j] == table_id[t]
                spots[j] = jnp.where(same, t, spots[j])
                found = jnp.where(same, b * KHOP + j, found)
            back[t][b] = found
        where_from[b] = spots

    gain_row = gain[...]

    for t in range(BLK):
        u, istd = layer_norm(x[t])
        unit[t * BS:(t + 1) * BS, :] = u
        inv[t * BS:(t + 1) * BS, :] = istd
        normed = (u * gain_row).astype(BF16)
        normed_t[:, t * BS:(t + 1) * BS] = normed.T
        q[t] = dot(normed, w[:, :d], ((1,), (0,))).astype(BF16)
        kv[t] = dot(normed, w[:, d:], ((1,), (0,))).astype(BF16)
    for s in range(2):
        terms[s, none] = jnp.zeros(terms.shape[2:], F32)
    ret[CAP * len(OFFSETS)] = jnp.zeros(ret.shape[1:], BF16)

    for oi in (1, 2, 0, 3):
        @pl.when(exists(oi))
        def _():
            halo_arrival(oi).wait_recv()
        for slot in range(CAP):
            t = BLK + CAP * oi + slot
            u, _istd = layer_norm(halo[oi, slot])
            unit[t * BS:(t + 1) * BS, :] = u
            normed = (u * gain_row).astype(BF16)
            normed_t[:, t * BS:(t + 1) * BS] = normed.T
            kv[t] = dot(normed, w[:, d:], ((1,), (0,))).astype(BF16)

    if fused_sum:
        (chunk, sib, parts, gchunk, gsib, gparts, done, gdone,
         sib_ss, sib_rs, part_ss, part_rs, done_ss, done_rs) = scratch[17:]

        def bufs(c):
            if c < HEADS:
                return chunk.at[c], sib.at[c], parts.at[c], done.at[c]
            return gchunk, gsib, gparts, gdone

        def to_sibling(c):
            mine_c, sib_c, _parts, _done = bufs(c)
            return pltpu.make_async_remote_copy(
                src_ref=mine_c, dst_ref=sib_c, send_sem=sib_ss.at[c], recv_sem=sib_rs.at[c],
                device_id={"noise": 1 - core}, device_id_type=MESH)

        def to_peer(c, k):
            mine_c, _sib, parts_c, _done = bufs(c)
            peer = lax.rem(me + k, n)
            return pltpu.make_async_remote_copy(
                src_ref=mine_c.at[pl.ds(pl.multiple_of(peer * rows_out, rows_out), rows_out), :],
                dst_ref=parts_c.at[k], send_sem=part_ss.at[c, k], recv_sem=part_rs.at[c, k],
                device_id={"mesh": peer}, device_id_type=MESH)

        def final_copy(c):
            _mine, _sib, _parts, done_c = bufs(c)
            return pltpu.make_async_remote_copy(
                src_ref=done_c, dst_ref=done_c, send_sem=done_ss.at[c], recv_sem=done_rs.at[c],
                device_id={"noise": 1 - core}, device_id_type=MESH)

        def begin(c):
            @pl.when(core != c % 2)
            def _():
                to_sibling(c).start()

        def spread(c):
            @pl.when(core == c % 2)
            def _():
                mine_c, sib_c, parts_c, _done = bufs(c)
                to_sibling(c).wait_recv()
                total = mine_c[...].astype(F32) + sib_c[...].astype(F32)
                mine_c[...] = total.astype(BF16)
                for k in range(1, n):
                    to_peer(c, k).start()

        def gather(c):
            @pl.when(core == c % 2)
            def _():
                mine_c, _sib, parts_c, done_c = bufs(c)
                total = mine_c[pl.ds(pl.multiple_of(me * rows_out, rows_out), rows_out), :].astype(F32)
                for k in range(1, n):
                    to_peer(c, k).wait_recv()
                    total = total + parts_c[k].astype(F32)
                done_c[...] = total
                final_copy(c).start()

        def finish(c):
            @pl.when(core == c % 2)
            def _():
                final_copy(c).wait_send()
                for k in range(1, n):
                    to_peer(c, k).wait_send()

            @pl.when(core != c % 2)
            def _():
                to_sibling(c).wait_send()
                final_copy(c).wait_recv()
            _mine, _sib, _parts, done_c = bufs(c)
            if c < HEADS:
                for part in range(3):
                    w_out[:, part * d + c * hd:part * d + (c + 1) * hd] = done_c[:, part * hd:(part + 1) * hd]
            else:
                gain_out[...] = done_c[...]

    for h in range(HEADS):
        lo, hi = h * hd, (h + 1) * hd
        buf = h % 2
        for b in range(BLK):
            kg = jnp.concatenate([kv[where_from[b][j], :, lo:hi] for j in range(KHOP)], axis=0)
            vg = jnp.concatenate([kv[where_from[b][j], :, d + lo:d + hi] for j in range(KHOP)], axis=0)
            qh = q[b, :, lo:hi]
            gh = og[b, :, lo:hi]
            s = dot(kg, qh, ((1,), (1,)))
            top = jnp.max(s, axis=0, keepdims=True)
            p = jnp.exp2((s - top) * (scale * math.log2(math.e)))
            a = p * (1.0 / jnp.sum(p, axis=0, keepdims=True))
            a_low = a.astype(BF16)
            da = dot(vg, gh, ((1,), (1,)))
            row_dot = jnp.sum(a_low.astype(F32) * da, axis=0, keepdims=True)
            ds = (a * (da - row_dot)).astype(BF16)
            dq[b * BS:(b + 1) * BS, lo:hi] = (dot(ds, kg, ((0,), (0,))) * scale).astype(BF16)
            dk = dot(ds, qh, ((1,), (0,))) * scale
            dv = dot(a_low, gh, ((1,), (0,)))
            for j in range(KHOP):
                terms[buf, b * KHOP + j, :, :hd] = dk[j * BS:(j + 1) * BS]
                terms[buf, b * KHOP + j, :, hd:] = dv[j * BS:(j + 1) * BS]
        for t in range(TABLE):
            total = terms[buf, back[t][0]]
            for b in range(1, BLK):
                total = total + terms[buf, back[t][b]]
            dkv[t * BS:(t + 1) * BS, lo:hi] = total[:, :hd].astype(BF16)
            dkv[t * BS:(t + 1) * BS, d + lo:d + hi] = total[:, hd:].astype(BF16)
        wq = dot(normed_t[:, :rows_dev], dq[:, lo:hi], ((1,), (0,))) * grad_scale
        kv_cols = jnp.concatenate([dkv[:, lo:hi], dkv[:, d + lo:d + hi]], axis=1)
        wkv = dot(normed_t[...], kv_cols, ((1,), (0,))) * grad_scale
        if fused_sum:
            chunk[h, :, :hd] = wq.astype(BF16)
            chunk[h, :, hd:] = wkv.astype(BF16)
            begin(h)
            if h >= 1:
                spread(h - 1)
        else:
            w_out[:, lo:hi] = wq
            w_out[:, d + lo:d + hi] = wkv[:, :hd]
            w_out[:, 2 * d + lo:2 * d + hi] = wkv[:, hd:]

    def ret_copy(oi):
        return pltpu.make_async_remote_copy(
            src_ref=ret_send.at[oi], dst_ref=ret.at[pl.ds(CAP * (3 - oi), CAP)],
            send_sem=ret_ss.at[oi], recv_sem=ret_rs.at[3 - oi],
            device_id={"mesh": me + OFFSETS[oi]}, device_id_type=MESH)

    def ret_arrival(oi):
        return pltpu.make_async_remote_copy(
            src_ref=ret_send.at[oi], dst_ref=ret.at[pl.ds(CAP * oi, CAP)],
            send_sem=ret_ss.at[oi], recv_sem=ret_rs.at[oi],
            device_id={"mesh": me + OFFSETS[oi]}, device_id_type=MESH)

    gain_sum = jnp.zeros((1, d), F32)
    for oi in (0, 3, 1, 2):
        r0 = (BLK + CAP * oi) * BS
        ng = dot(dkv[r0:r0 + CAP * BS, :], w[:, d:], ((1,), (1,)))
        gain_sum += jnp.sum(ng * unit[r0:r0 + CAP * BS, :], axis=0, keepdims=True)
        for slot in range(CAP):
            ret_send[oi, slot] = ng[slot * BS:(slot + 1) * BS].astype(BF16)

        @pl.when(exists(oi))
        def _():
            ret_copy(oi).start()
    if fused_sum:
        spread(HEADS - 1)
    ng = dot(dq[...], w[:, :d], ((1,), (1,))) + dot(dkv[:rows_dev, :], w[:, d:], ((1,), (1,)))
    own_ng[...] = ng
    gain_sum += jnp.sum(ng * unit[:rows_dev, :], axis=0, keepdims=True)
    gain_sum = gain_sum * grad_scale
    if fused_sum:
        gchunk[...] = jnp.broadcast_to(gain_sum, (BS, d)).T.astype(BF16)
        begin(HEADS)
        for c in range(HEADS - 1):
            gather(c)
        spread(HEADS)
    else:
        gain_out[...] = gain_sum

    for oi in range(len(OFFSETS)):
        @pl.when(exists(oi))
        def _():
            ret_arrival(oi).wait_recv()
    for c in range(BLK):
        total = own_ng[c * BS:(c + 1) * BS, :]
        for oi in range(len(OFFSETS)):
            flags, first, _second = wanted[oi]
            spot = CAP * oi + jnp.where(first == c, 0, 1)
            spot = jnp.where(jnp.logical_and(flags[c], exists(oi)), spot, CAP * len(OFFSETS))
            total = total + ret[spot].astype(F32)
        u = unit[c * BS:(c + 1) * BS, :]
        ug = total * gain_row
        mean = jnp.mean(ug, axis=-1, keepdims=True)
        along = jnp.mean(ug * u, axis=-1, keepdims=True)
        dx[c] = (inv[c * BS:(c + 1) * BS, :] * (ug - mean - u * along)).astype(BF16)

    if fused_sum:
        gather(HEADS - 1)
        gather(HEADS)
        for c in range(HEADS + 1):
            finish(c)
    for oi in range(len(OFFSETS)):
        @pl.when(exists(oi))
        def _():
            halo_copy(oi).wait_send()
            ret_copy(oi).wait_send()


def per_device(n, noise, inputs, norm_gain, qkv_weight, neighbours, out_grad):
    samples, row_count, d = inputs.shape
    hd = d // HEADS
    rows_out = d // n
    grad_scale = 1.0 / math.sqrt(samples * row_count * n * noise)
    fused_sum = n <= 8 and rows_out % 16 == 0 and noise == 2
    vmem = pl.BlockSpec(memory_space=pltpu.VMEM)
    offs = len(OFFSETS)
    scratch = [
        pltpu.VMEM((offs, CAP, BS, d), BF16),
        pltpu.VMEM((offs, CAP, BS, d), BF16),
        pltpu.VMEM((TABLE * BS, d), F32),
        pltpu.VMEM((row_count, 1), F32),
        pltpu.VMEM((d, TABLE * BS), BF16),
        pltpu.VMEM((BLK, BS, d), BF16),
        pltpu.VMEM((TABLE, BS, 2 * d), BF16),
        pltpu.VMEM((row_count, d), BF16),
        pltpu.VMEM((TABLE * BS, 2 * d), BF16),
        pltpu.VMEM((2, BLK * KHOP + 1, BS, 2 * hd), F32),
        pltpu.VMEM((row_count, d), F32),
        pltpu.VMEM((offs, CAP, BS, d), BF16),
        pltpu.VMEM((offs * CAP + 1, BS, d), BF16),
    ] + [pltpu.SemaphoreType.DMA((offs,))] * 4
    out_shape = [jax.ShapeDtypeStruct((BLK, BS, d), BF16)]
    if fused_sum:
        cw = 3 * hd
        scratch += [
            pltpu.VMEM((HEADS, d, cw), BF16),
            pltpu.VMEM((HEADS, d, cw), BF16),
            pltpu.VMEM((HEADS, n, rows_out, cw), BF16),
            pltpu.VMEM((d, BS), BF16),
            pltpu.VMEM((d, BS), BF16),
            pltpu.VMEM((n, rows_out, BS), BF16),
            pltpu.VMEM((HEADS, rows_out, cw), F32),
            pltpu.VMEM((rows_out, BS), F32),
            pltpu.SemaphoreType.DMA((HEADS + 1,)),
            pltpu.SemaphoreType.DMA((HEADS + 1,)),
            pltpu.SemaphoreType.DMA((HEADS + 1, n)),
            pltpu.SemaphoreType.DMA((HEADS + 1, n)),
            pltpu.SemaphoreType.DMA((HEADS + 1,)),
            pltpu.SemaphoreType.DMA((HEADS + 1,)),
        ]
        out_shape += [
            jax.ShapeDtypeStruct((rows_out, 3 * d), F32),
            jax.ShapeDtypeStruct((rows_out, BS), F32),
        ]
    else:
        out_shape += [
            jax.ShapeDtypeStruct((d, 3 * d), F32),
            jax.ShapeDtypeStruct((1, d), F32),
        ]
    dx, w_term, gain_term = pl.pallas_call(
        functools.partial(kernel, n, grad_scale, fused_sum),
        out_shape=out_shape,
        in_specs=[pl.BlockSpec(memory_space=pltpu.SMEM), vmem, vmem, vmem, vmem],
        out_specs=[vmem] * 3,
        scratch_shapes=scratch,
        compiler_params=pltpu.CompilerParams(
            collective_id=0, has_side_effects=True, vmem_limit_bytes=56 * 1024 * 1024
        ),
        cost_estimate=pl.CostEstimate(
            flops=8_000_000_000, bytes_accessed=6_000_000, transcendentals=2_000_000
        ),
    )(
        neighbours,
        inputs.reshape(BLK, BS, d),
        norm_gain.reshape(1, d),
        qkv_weight,
        out_grad.reshape(BLK, BS, d),
    )
    input_grad = dx.reshape(inputs.shape)
    if fused_sum:
        return input_grad, w_term, gain_term[:, 0]
    weight_all = lax.psum(w_term.astype(BF16), "noise").astype(F32)
    gain_all = lax.psum(gain_term[0].astype(BF16), "noise").astype(F32)
    return (
        input_grad,
        lax.psum_scatter(weight_all, "mesh", scatter_dimension=0, tiled=True),
        lax.psum_scatter(gain_all, "mesh", scatter_dimension=0, tiled=True),
    )


def solution(mesh):
    return jax.shard_map(
        functools.partial(per_device, mesh.shape["mesh"], mesh.shape["noise"]),
        mesh=mesh,
        in_specs=(
            P(("groups", "noise"), "mesh", None),
            P(),
            P(),
            P(),
            P(("groups", "noise"), "mesh", None),
        ),
        out_specs=(
            P(("groups", "noise"), "mesh", None),
            P(("groups", "mesh"), None),
            P(("groups", "mesh")),
        ),
        check_vma=False,
    )
```

time: 333 us -> 74.9 us (0.22)
  waiting for transfers between devices: 144 us -> 0 us
  Pallas kernels: 0 us -> 67.5 us
  local copies, waits for them, and re-layouts: 60 us -> 6.39 us
  matrix products: 53.6 us -> 0 us
  blocking collectives: 24.4 us -> 0 us
  starting transfers between devices: 23.2 us -> 0 us
  between operations: 14.9 us -> 0.64 us
  other arithmetic: 10.9 us -> 0 us
    ppermute x8 -> x0, waiting for transfers between devices: 80.6 us -> none  [shifted(): return lax.ppermute(block, axis, route)]
    pallas_call x0 -> x1, Pallas kernels: none -> 67.5 us  [per_device(): pl.pallas_call(functools.partial(kernel, n, grad_scale, fused_sum), out_s...]
    dot_general x31 -> x0, matrix products: 53.6 us -> none  [the longest x4 34.8 us: per_head(): jnp.einsum('bjt,sbjkcd->stkcd', table_hits, pair_grad, precision=lax.Prec...]
    reduce_scatter x1 -> x0, waiting for transfers between devices: 46.1 us -> none  [per_device(): lax.psum_scatter(weight_all, 'mesh', scatter_dimension=0, tiled=True)]
    ppermute x8 -> x0, starting transfers between devices: 23.2 us -> none  [shifted(): return lax.ppermute(block, axis, route)]
    unnamed x1 -> x0, blocking collectives: 21.9 us -> none
    psum x1 -> x0, waiting for transfers between devices: 17.8 us -> none  [per_device(): lax.psum(weight_term.astype(jnp.bfloat16), 'noise').astype(jnp.float32)]
    gather x8 -> x0, local copies, waits for them, and re-layouts: 14.2 us -> none  [per_head(): gathered = pair_head[:, where_from]]
  transfers between devices with their start and end apart: 10 -> 0, of which waited for: 7 -> 0; matrix products, arithmetic and copies ran while one was open for 5% -> 0% of each run, Pallas kernels for 0% -> 0%
where the time goes in v1:
time: 74.9 us; the launch traced here: 74.6 us
  Pallas kernels  67.5 us (90%)
  local copies, waits for them, and re-layouts  6.39 us (9%)
    pallas_call x1, Pallas kernels, per_device(): pl.pallas_call(functools.partial(kernel, n, grad_scale, fused_sum), out_s...  67.5 us
    unnamed x3, local copies, waits for them, and re-layouts  5.01 us

profile of v1, /device:TPU:0, one launch (start us, length us, event | category | flops | bytes accessed | tf_op | source)
XLA Modules:
  0.0 74.6 jit_solution(1288885461921705016)
XLA Ops:
  0.6 1.4 %copy.9.neigh = s32[32,6]{1,0:T(8,128)} copy(s32[32,6]{0,1:T(8,128)} %param.8) | data formatting | bytes 1536 | tf_op args[3]
  2.0 67.5 %shard_map.76 = (bf16[4,128,512]{2,1,0:T(8,128)(2,1)}, f32[64,1536]{1,0:T(8,128)}, f32[64,128]{1,0:T(8,128)}) custom-call(s32[32,6]{1,0:T(8,128)} %copy.9.neigh, bf16[4,128,512]{2,1,0:T(8,128)(2,1)} %bitcast.5, f32[1,512]{1,0:T(1,128)} %bitcast.7, bf16[512,1536]{1,0:T(8,128)(2,1)} %w.1, bf16[4,128,512]{2,1,0:T(8,128)(2,1)} %bitcast.6), custom_call_target="tpu_custom_call" | custom-call | flops 8000000000 | bytes 6000000 | tf_op jit(solution)/shard_map/pallas_call | solution.py:408
  69.5 1.4 %slice_reduce_fusion = f32[64]{0:T(128)} fusion(f32[64,128]{1,0:T(8,128)} %get-tuple-element.8), kind=kLoop, calls=%fused_computation | loop fusion | bytes 512 | tf_op jit(solution)/shard_map/slice | solution.py:429
  70.9 1.9 %copy.12 = bf16[1,512,512]{2,1,0:T(8,128)(2,1)} copy(bf16[1,512,512]{2,1,0:T(8,128)(2,1)} %bitcast.4) | data formatting | bytes 1048576
  72.8 1.8 %copy.13 = f32[64,1536]{1,0:T(8,128)} copy(f32[64,1536]{1,0:T(8,128)} %get-tuple-element.13) | data formatting | bytes 786432

commit v2 on v1

--- a/solution.py
+++ b/solution.py
@@ -54,20 +54,30 @@
 
 def kernel(
     n, grad_scale, fused_sum,
-    neigh, x, gain, w, og,
+    neigh_any, x_any, gain, w_any, og_any,
     *refs,
 ):
     outs, scratch = refs[:3], refs[3:]
     dx, w_out, gain_out = outs
     (send, halo, unit, inv, normed_t, q, kv, dq, dkv, terms, own_ng, ret_send, ret,
-     halo_ss, halo_rs, ret_ss, ret_rs) = scratch[:17]
+     halo_ss, halo_rs, ret_ss, ret_rs, neigh, x, w, og, dx_v, in_sem, dx_sem) = scratch[:24]
+    loads = [
+        pltpu.make_async_copy(src, dst, in_sem.at[i])
+        for i, (src, dst) in enumerate(((neigh_any, neigh), (x_any, x), (w_any, w), (og_any, og)))
+    ]
+    for load in loads:
+        load.start()
     me = lax.axis_index("mesh")
     core = lax.axis_index("noise")
-    d = x.shape[-1]
+    d = x_any.shape[-1]
     hd = d // HEADS
     rows_dev = BLK * BS
     scale = 1.0 / math.sqrt(hd)
     rows_out = d // n
+    side = lax.rem(me, 2)
+    plane = me // 2
+    planes = n // 2
+    beside = me + 1 - 2 * side
 
     def exists(oi):
         other = me + OFFSETS[oi]
@@ -78,11 +88,16 @@
         for k in range(1, n):
             pl.semaphore_signal(barrier, inc=1, device_id={"mesh": lax.rem(me + k, n)}, device_id_type=MESH)
         pl.semaphore_signal(barrier, inc=1, device_id={"noise": 1 - core}, device_id_type=MESH)
+        pl.semaphore_signal(
+            barrier, inc=1, device_id={"mesh": beside, "noise": 1 - core}, device_id_type=MESH)
     else:
         for oi in range(len(OFFSETS)):
             @pl.when(exists(oi))
             def _():
                 pl.semaphore_signal(barrier, inc=1, device_id={"mesh": me + OFFSETS[oi]}, device_id_type=MESH)
+
+    loads[0].wait()
+    loads[1].wait()
 
     wanted = []
     for oi, off in enumerate(OFFSETS):
@@ -95,7 +110,7 @@
         send[oi, 1] = x[second]
 
     if fused_sum:
-        pl.semaphore_wait(barrier, n)
+        pl.semaphore_wait(barrier, n + 1)
     else:
         for oi in range(len(OFFSETS)):
             @pl.when(exists(oi))
@@ -148,55 +163,63 @@
 
     gain_row = gain[...]
 
-    for t in range(BLK):
-        u, istd = layer_norm(x[t])
-        unit[t * BS:(t + 1) * BS, :] = u
-        inv[t * BS:(t + 1) * BS, :] = istd
-        normed = (u * gain_row).astype(BF16)
-        normed_t[:, t * BS:(t + 1) * BS] = normed.T
-        q[t] = dot(normed, w[:, :d], ((1,), (0,))).astype(BF16)
-        kv[t] = dot(normed, w[:, d:], ((1,), (0,))).astype(BF16)
+    u, istd = layer_norm(x[...].reshape(rows_dev, d))
+    unit[:rows_dev, :] = u
+    inv[...] = istd
+    normed = (u * gain_row).astype(BF16)
+    loads[2].wait()
+    q[...] = dot(normed, w[:, :d], ((1,), (0,))).astype(BF16).reshape(BLK, BS, d)
+    kv[:BLK] = dot(normed, w[:, d:], ((1,), (0,))).astype(BF16).reshape(BLK, BS, 2 * d)
+    normed_t[:, :rows_dev] = normed.T
+    loads[3].wait()
     for s in range(2):
         terms[s, none] = jnp.zeros(terms.shape[2:], F32)
     ret[CAP * len(OFFSETS)] = jnp.zeros(ret.shape[1:], BF16)
 
-    for oi in (1, 2, 0, 3):
+    for oi in (0, 3, 1, 2):
         @pl.when(exists(oi))
         def _():
             halo_arrival(oi).wait_recv()
-        for slot in range(CAP):
-            t = BLK + CAP * oi + slot
-            u, _istd = layer_norm(halo[oi, slot])
-            unit[t * BS:(t + 1) * BS, :] = u
-            normed = (u * gain_row).astype(BF16)
-            normed_t[:, t * BS:(t + 1) * BS] = normed.T
-            kv[t] = dot(normed, w[:, d:], ((1,), (0,))).astype(BF16)
-
-    if fused_sum:
-        (chunk, sib, parts, gchunk, gsib, gparts, done, gdone,
-         sib_ss, sib_rs, part_ss, part_rs, done_ss, done_rs) = scratch[17:]
+        t = BLK + CAP * oi
+        u, _istd = layer_norm(halo[oi].reshape(CAP * BS, d))
+        unit[t * BS:(t + CAP) * BS, :] = u
+        normed = (u * gain_row).astype(BF16)
+        kv[t:t + CAP] = dot(normed, w[:, d:], ((1,), (0,))).astype(BF16).reshape(CAP, BS, 2 * d)
+        normed_t[:, t * BS:(t + CAP) * BS] = normed.T
+
+    if fused_sum:
+        (chunk, quad, held, parts, gchunk, gquad, gheld, gparts, done, gdone,
+         quad_ss, quad_rs, part_ss, part_rs, done_ss, done_rs) = scratch[24:]
 
         def bufs(c):
             if c < HEADS:
-                return chunk.at[c], sib.at[c], parts.at[c], done.at[c]
-            return gchunk, gsib, gparts, gdone
-
-        def to_sibling(c):
-            mine_c, sib_c, _parts, _done = bufs(c)
+                return chunk.at[c], quad.at[c], held.at[c], parts.at[c], done.at[c]
+            return gchunk, gquad, gheld, gparts, gdone
+
+        def quad_copy(c, to_side, device, place):
             return pltpu.make_async_remote_copy(
-                src_ref=mine_c, dst_ref=sib_c, send_sem=sib_ss.at[c], recv_sem=sib_rs.at[c],
-                device_id={"noise": 1 - core}, device_id_type=MESH)
-
-        def to_peer(c, k):
-            mine_c, _sib, parts_c, _done = bufs(c)
-            peer = lax.rem(me + k, n)
+                src_ref=bufs(c)[0].at[to_side], dst_ref=bufs(c)[1].at[place],
+                send_sem=quad_ss.at[c, place], recv_sem=quad_rs.at[c, place],
+                device_id=device, device_id_type=MESH)
+
+        def from_sibling(c):
+            return quad_copy(c, side, {"noise": 1 - core}, 0)
+
+        def from_beside(c):
+            return quad_copy(c, 1 - side, {"mesh": beside}, 1)
+
+        def from_across(c):
+            return quad_copy(c, 1 - side, {"mesh": beside, "noise": 1 - core}, 2)
+
+        def to_plane(c, k):
+            _chunk, _quad, held_c, parts_c, _done = bufs(c)
             return pltpu.make_async_remote_copy(
-                src_ref=mine_c.at[pl.ds(pl.multiple_of(peer * rows_out, rows_out), rows_out), :],
+                src_ref=held_c.at[lax.rem(plane + k, planes)],
                 dst_ref=parts_c.at[k], send_sem=part_ss.at[c, k], recv_sem=part_rs.at[c, k],
-                device_id={"mesh": peer}, device_id_type=MESH)
+                device_id={"mesh": lax.rem(me + 2 * k, n)}, device_id_type=MESH)
 
         def final_copy(c):
-            _mine, _sib, _parts, done_c = bufs(c)
+            done_c = bufs(c)[4]
             return pltpu.make_async_remote_copy(
                 src_ref=done_c, dst_ref=done_c, send_sem=done_ss.at[c], recv_sem=done_rs.at[c],
                 device_id={"noise": 1 - core}, device_id_type=MESH)
@@ -204,25 +227,34 @@
         def begin(c):
             @pl.when(core != c % 2)
             def _():
-                to_sibling(c).start()
+                from_across(c).start()
+                from_sibling(c).start()
+
+            @pl.when(core == c % 2)
+            def _():
+                from_beside(c).start()
 
         def spread(c):
             @pl.when(core == c % 2)
             def _():
-                mine_c, sib_c, parts_c, _done = bufs(c)
-                to_sibling(c).wait_recv()
-                total = mine_c[...].astype(F32) + sib_c[...].astype(F32)
-                mine_c[...] = total.astype(BF16)
-                for k in range(1, n):
-                    to_peer(c, k).start()
+                chunk_c, quad_c, held_c, _parts, _done = bufs(c)
+                from_sibling(c).wait_recv()
+                from_beside(c).wait_recv()
+                from_across(c).wait_recv()
+                total = chunk_c[side].astype(F32)
+                for place in range(3):
+                    total = total + quad_c[place].astype(F32)
+                held_c[...] = total.astype(BF16)
+                for k in range(1, planes):
+                    to_plane(c, k).start()
 
         def gather(c):
             @pl.when(core == c % 2)
             def _():
-                mine_c, _sib, parts_c, done_c = bufs(c)
-                total = mine_c[pl.ds(pl.multiple_of(me * rows_out, rows_out), rows_out), :].astype(F32)
-                for k in range(1, n):
-                    to_peer(c, k).wait_recv()
+                _chunk, _quad, held_c, parts_c, done_c = bufs(c)
+                total = held_c[plane].astype(F32)
+                for k in range(1, planes):
+                    to_plane(c, k).wait_recv()
                     total = total + parts_c[k].astype(F32)
                 done_c[...] = total
                 final_copy(c).start()
@@ -231,19 +263,38 @@
             @pl.when(core == c % 2)
             def _():
                 final_copy(c).wait_send()
-                for k in range(1, n):
-                    to_peer(c, k).wait_send()
+                from_beside(c).wait_send()
+                for k in range(1, planes):
+                    to_plane(c, k).wait_send()
 
             @pl.when(core != c % 2)
             def _():
-                to_sibling(c).wait_send()
+                from_across(c).wait_send()
+                from_sibling(c).wait_send()
                 final_copy(c).wait_recv()
-            _mine, _sib, _parts, done_c = bufs(c)
+            done_c = bufs(c)[4]
             if c < HEADS:
                 for part in range(3):
                     w_out[:, part * d + c * hd:part * d + (c + 1) * hd] = done_c[:, part * hd:(part + 1) * hd]
             else:
                 gain_out[...] = done_c[...]
+
+    def weight_product(h):
+        lo, hi = h * hd, (h + 1) * hd
+        wq = dot(normed_t[:, :rows_dev], dq[:, lo:hi], ((1,), (0,))) * grad_scale
+        kv_cols = jnp.concatenate([dkv[:, lo:hi], dkv[:, d + lo:d + hi]], axis=1)
+        wkv = dot(normed_t[...], kv_cols, ((1,), (0,))) * grad_scale
+        if fused_sum:
+            wq, wkv = wq.astype(BF16), wkv.astype(BF16)
+            for p in range(n):
+                rows = slice(p * rows_out, (p + 1) * rows_out)
+                chunk[h, p % 2, p // 2, :, :hd] = wq[rows]
+                chunk[h, p % 2, p // 2, :, hd:] = wkv[rows]
+            begin(h)
+        else:
+            w_out[:, lo:hi] = wq
+            w_out[:, d + lo:d + hi] = wkv[:, :hd]
+            w_out[:, 2 * d + lo:2 * d + hi] = wkv[:, hd:]
 
     for h in range(HEADS):
         lo, hi = h * hd, (h + 1) * hd
@@ -273,19 +324,10 @@
                 total = total + terms[buf, back[t][b]]
             dkv[t * BS:(t + 1) * BS, lo:hi] = total[:, :hd].astype(BF16)
             dkv[t * BS:(t + 1) * BS, d + lo:d + hi] = total[:, hd:].astype(BF16)
-        wq = dot(normed_t[:, :rows_dev], dq[:, lo:hi], ((1,), (0,))) * grad_scale
-        kv_cols = jnp.concatenate([dkv[:, lo:hi], dkv[:, d + lo:d + hi]], axis=1)
-        wkv = dot(normed_t[...], kv_cols, ((1,), (0,))) * grad_scale
-        if fused_sum:
-            chunk[h, :, :hd] = wq.astype(BF16)
-            chunk[h, :, hd:] = wkv.astype(BF16)
-            begin(h)
-            if h >= 1:
-                spread(h - 1)
-        else:
-            w_out[:, lo:hi] = wq
-            w_out[:, d + lo:d + hi] = wkv[:, :hd]
-            w_out[:, 2 * d + lo:2 * d + hi] = wkv[:, hd:]
+        if h < HEADS - 1:
+            weight_product(h)
+        if fused_sum and h >= 1:
+            spread(h - 1)
 
     def ret_copy(oi):
         return pltpu.make_async_remote_copy(
@@ -310,17 +352,20 @@
         @pl.when(exists(oi))
         def _():
             ret_copy(oi).start()
-    if fused_sum:
-        spread(HEADS - 1)
+    weight_product(HEADS - 1)
     ng = dot(dq[...], w[:, :d], ((1,), (1,))) + dot(dkv[:rows_dev, :], w[:, d:], ((1,), (1,)))
     own_ng[...] = ng
     gain_sum += jnp.sum(ng * unit[:rows_dev, :], axis=0, keepdims=True)
     gain_sum = gain_sum * grad_scale
     if fused_sum:
-        gchunk[...] = jnp.broadcast_to(gain_sum, (BS, d)).T.astype(BF16)
+        column = jnp.broadcast_to(gain_sum, (BS, d)).T.astype(BF16)
+        for p in range(n):
+            gchunk[p % 2, p // 2] = column[p * rows_out:(p + 1) * rows_out]
         begin(HEADS)
-        for c in range(HEADS - 1):
+        for c in range(HEADS - 2):
             gather(c)
+        spread(HEADS - 1)
+        gather(HEADS - 2)
         spread(HEADS)
     else:
         gain_out[...] = gain_sum
@@ -340,8 +385,10 @@
         ug = total * gain_row
         mean = jnp.mean(ug, axis=-1, keepdims=True)
         along = jnp.mean(ug * u, axis=-1, keepdims=True)
-        dx[c] = (inv[c * BS:(c + 1) * BS, :] * (ug - mean - u * along)).astype(BF16)
-
+        dx_v[c] = (inv[c * BS:(c + 1) * BS, :] * (ug - mean - u * along)).astype(BF16)
+
+    dx_copy = pltpu.make_async_copy(dx_v, dx, dx_sem)
+    dx_copy.start()
     if fused_sum:
         gather(HEADS - 1)
         gather(HEADS)
@@ -352,6 +399,7 @@
         def _():
             halo_copy(oi).wait_send()
             ret_copy(oi).wait_send()
+    dx_copy.wait()
 
 
 def per_device(n, noise, inputs, norm_gain, qkv_weight, neighbours, out_grad):
@@ -359,8 +407,9 @@
     hd = d // HEADS
     rows_out = d // n
     grad_scale = 1.0 / math.sqrt(samples * row_count * n * noise)
-    fused_sum = n <= 8 and rows_out % 16 == 0 and noise == 2
+    fused_sum = n <= 8 and n % 2 == 0 and rows_out % 16 == 0 and noise == 2
     vmem = pl.BlockSpec(memory_space=pltpu.VMEM)
+    anywhere = pl.BlockSpec(memory_space=pl.ANY)
     offs = len(OFFSETS)
     scratch = [
         pltpu.VMEM((offs, CAP, BS, d), BF16),
@@ -376,23 +425,33 @@
         pltpu.VMEM((row_count, d), F32),
         pltpu.VMEM((offs, CAP, BS, d), BF16),
         pltpu.VMEM((offs * CAP + 1, BS, d), BF16),
-    ] + [pltpu.SemaphoreType.DMA((offs,))] * 4
+    ] + [pltpu.SemaphoreType.DMA((offs,))] * 4 + [
+        pltpu.SMEM(neighbours.shape, jnp.int32),
+        pltpu.VMEM((BLK, BS, d), BF16),
+        pltpu.VMEM((d, 3 * d), BF16),
+        pltpu.VMEM((BLK, BS, d), BF16),
+        pltpu.VMEM((BLK, BS, d), BF16),
+        pltpu.SemaphoreType.DMA((4,)),
+        pltpu.SemaphoreType.DMA,
+    ]
     out_shape = [jax.ShapeDtypeStruct((BLK, BS, d), BF16)]
     if fused_sum:
         cw = 3 * hd
         scratch += [
-            pltpu.VMEM((HEADS, d, cw), BF16),
-            pltpu.VMEM((HEADS, d, cw), BF16),
-            pltpu.VMEM((HEADS, n, rows_out, cw), BF16),
-            pltpu.VMEM((d, BS), BF16),
-            pltpu.VMEM((d, BS), BF16),
-            pltpu.VMEM((n, rows_out, BS), BF16),
+            pltpu.VMEM((HEADS, 2, n // 2, rows_out, cw), BF16),
+            pltpu.VMEM((HEADS, 3, n // 2, rows_out, cw), BF16),
+            pltpu.VMEM((HEADS, n // 2, rows_out, cw), BF16),
+            pltpu.VMEM((HEADS, n // 2, rows_out, cw), BF16),
+            pltpu.VMEM((2, n // 2, rows_out, BS), BF16),
+            pltpu.VMEM((3, n // 2, rows_out, BS), BF16),
+            pltpu.VMEM((n // 2, rows_out, BS), BF16),
+            pltpu.VMEM((n // 2, rows_out, BS), BF16),
             pltpu.VMEM((HEADS, rows_out, cw), F32),
             pltpu.VMEM((rows_out, BS), F32),
-            pltpu.SemaphoreType.DMA((HEADS + 1,)),
-            pltpu.SemaphoreType.DMA((HEADS + 1,)),
-            pltpu.SemaphoreType.DMA((HEADS + 1, n)),
-            pltpu.SemaphoreType.DMA((HEADS + 1, n)),
+            pltpu.SemaphoreType.DMA((HEADS + 1, 3)),
+            pltpu.SemaphoreType.DMA((HEADS + 1, 3)),
+            pltpu.SemaphoreType.DMA((HEADS + 1, n // 2)),
+            pltpu.SemaphoreType.DMA((HEADS + 1, n // 2)),
             pltpu.SemaphoreType.DMA((HEADS + 1,)),
             pltpu.SemaphoreType.DMA((HEADS + 1,)),
         ]
@@ -408,8 +467,8 @@
     dx, w_term, gain_term = pl.pallas_call(
         functools.partial(kernel, n, grad_scale, fused_sum),
         out_shape=out_shape,
-        in_specs=[pl.BlockSpec(memory_space=pltpu.SMEM), vmem, vmem, vmem, vmem],
-        out_specs=[vmem] * 3,
+        in_specs=[anywhere, anywhere, vmem, anywhere, anywhere],
+        out_specs=[anywhere, vmem, vmem],
         scratch_shapes=scratch,
         compiler_params=pltpu.CompilerParams(
             collective_id=0, has_side_effects=True, vmem_limit_bytes=56 * 1024 * 1024

time: 74.9 us -> 72.6 us (0.969)
  Pallas kernels: 67.5 us -> 65.3 us
    pallas_call x1, Pallas kernels: 67.5 us -> 65.3 us  [per_device(): pl.pallas_call(functools.partial(kernel, n, grad_scale, fused_sum), out_s...]
where the time goes in v2:
time: 72.6 us; the launch traced here: 72.3 us
  Pallas kernels  65.3 us (90%)
  local copies, waits for them, and re-layouts  6.39 us (9%)
    pallas_call x1, Pallas kernels, per_device(): pl.pallas_call(functools.partial(kernel, n, grad_scale, fused_sum), out_s...  65.3 us
    unnamed x3, local copies, waits for them, and re-layouts  5.01 us

profile of v2, /device:TPU:0, one launch (start us, length us, event | category | flops | bytes accessed | tf_op | source)
XLA Modules:
  0.0 72.3 jit_solution(16378766389337590936)
XLA Ops:
  0.6 1.4 %copy.9.neigh_any = s32[32,6]{1,0:T(8,128)} copy(s32[32,6]{0,1:T(8,128)} %param.8) | data formatting | bytes 1536 | tf_op args[3]
  2.0 65.3 %shard_map.76 = (bf16[4,128,512]{2,1,0:T(8,128)(2,1)}, f32[64,1536]{1,0:T(8,128)}, f32[64,128]{1,0:T(8,128)}) custom-call(s32[32,6]{1,0:T(8,128)} %copy.9.neigh_any, bf16[4,128,512]{2,1,0:T(8,128)(2,1)} %bitcast.5, f32[1,512]{1,0:T(1,128)} %bitcast.7, bf16[512,1536]{1,0:T(8,128)(2,1)} %w_any.1, bf16[4,128,512]{2,1,0:T(8,128)(2,1)} %bitcast.6), custom_call_target="tpu_custom_call" | custom-call | flops 8000000000 | bytes 6000000 | tf_op jit(solution)/shard_map/pallas_call | solution.py:467
  67.3 1.4 %slice_reduce_fusion = f32[64]{0:T(128)} fusion(f32[64,128]{1,0:T(8,128)} %get-tuple-element.8), kind=kLoop, calls=%fused_computation | loop fusion | bytes 512 | tf_op jit(solution)/shard_map/slice | solution.py:488
  68.7 1.9 %copy.12 = bf16[1,512,512]{2,1,0:T(8,128)(2,1)} copy(bf16[1,512,512]{2,1,0:T(8,128)(2,1)} %bitcast.4) | data formatting | bytes 1048576
  70.5 1.8 %copy.13 = f32[64,1536]{1,0:T(8,128)} copy(f32[64,1536]{1,0:T(8,128)} %get-tuple-element.13) | data formatting | bytes 786432

commit v3 on v2

--- a/solution.py
+++ b/solution.py
@@ -324,8 +324,7 @@
                 total = total + terms[buf, back[t][b]]
             dkv[t * BS:(t + 1) * BS, lo:hi] = total[:, :hd].astype(BF16)
             dkv[t * BS:(t + 1) * BS, d + lo:d + hi] = total[:, hd:].astype(BF16)
-        if h < HEADS - 1:
-            weight_product(h)
+        weight_product(h)
         if fused_sum and h >= 1:
             spread(h - 1)
 
@@ -352,7 +351,6 @@
         @pl.when(exists(oi))
         def _():
             ret_copy(oi).start()
-    weight_product(HEADS - 1)
     ng = dot(dq[...], w[:, :d], ((1,), (1,))) + dot(dkv[:rows_dev, :], w[:, d:], ((1,), (1,)))
     own_ng[...] = ng
     gain_sum += jnp.sum(ng * unit[:rows_dev, :], axis=0, keepdims=True)
@@ -362,11 +360,12 @@
         for p in range(n):
             gchunk[p % 2, p // 2] = column[p * rows_out:(p + 1) * rows_out]
         begin(HEADS)
-        for c in range(HEADS - 2):
+        spread(HEADS - 1)
+        for c in range(HEADS - 1):
             gather(c)
-        spread(HEADS - 1)
-        gather(HEADS - 2)
         spread(HEADS)
+        for c in range(HEADS - 1):
+            finish(c)
     else:
         gain_out[...] = gain_sum
 
@@ -392,7 +391,7 @@
     if fused_sum:
         gather(HEADS - 1)
         gather(HEADS)
-        for c in range(HEADS + 1):
+        for c in (HEADS - 1, HEADS):
             finish(c)
     for oi in range(len(OFFSETS)):
         @pl.when(exists(oi))

time: 72.6 us -> 71.8 us (0.989)
  Pallas kernels: 65.3 us -> 64.5 us
    pallas_call x1, Pallas kernels: 65.3 us -> 64.5 us  [per_device(): pl.pallas_call(functools.partial(kernel, n, grad_scale, fused_sum), out_s...]
where the time goes in v3:
time: 71.8 us; the launch traced here: 71.5 us
  Pallas kernels  64.5 us (90%)
  local copies, waits for them, and re-layouts  6.39 us (9%)
    pallas_call x1, Pallas kernels, per_device(): pl.pallas_call(functools.partial(kernel, n, grad_scale, fused_sum), out_s...  64.5 us
    unnamed x3, local copies, waits for them, and re-layouts  5.01 us

profile of v3, /device:TPU:0, one launch (start us, length us, event | category | flops | bytes accessed | tf_op | source)
XLA Modules:
  0.0 71.5 jit_solution(2857405281054273460)
XLA Ops:
  0.6 1.4 %copy.9.neigh_any = s32[32,6]{1,0:T(8,128)} copy(s32[32,6]{0,1:T(8,128)} %param.8) | data formatting | bytes 1536 | tf_op args[3]
  2.0 64.5 %shard_map.76 = (bf16[4,128,512]{2,1,0:T(8,128)(2,1)}, f32[64,1536]{1,0:T(8,128)}, f32[64,128]{1,0:T(8,128)}) custom-call(s32[32,6]{1,0:T(8,128)} %copy.9.neigh_any, bf16[4,128,512]{2,1,0:T(8,128)(2,1)} %bitcast.5, f32[1,512]{1,0:T(1,128)} %bitcast.7, bf16[512,1536]{1,0:T(8,128)(2,1)} %w_any.1, bf16[4,128,512]{2,1,0:T(8,128)(2,1)} %bitcast.6), custom_call_target="tpu_custom_call" | custom-call | flops 8000000000 | bytes 6000000 | tf_op jit(solution)/shard_map/pallas_call | solution.py:466
  66.5 1.4 %slice_reduce_fusion = f32[64]{0:T(128)} fusion(f32[64,128]{1,0:T(8,128)} %get-tuple-element.8), kind=kLoop, calls=%fused_computation | loop fusion | bytes 512 | tf_op jit(solution)/shard_map/slice | solution.py:487
  67.8 1.9 %copy.12 = bf16[1,512,512]{2,1,0:T(8,128)(2,1)} copy(bf16[1,512,512]{2,1,0:T(8,128)(2,1)} %bitcast.4) | data formatting | bytes 1048576
  69.7 1.8 %copy.13 = f32[64,1536]{1,0:T(8,128)} copy(f32[64,1536]{1,0:T(8,128)} %get-tuple-element.13) | data formatting | bytes 786432
